TPU v7x, 512 devices: a whole 4x4x16 slice. The times are simulated.
512 devices in a mesh: snap: 16 (over x, y), vert: 32 (over z, core).
Axes of the slice: x: 4, y: 4, z: 16, core: 2. Of those that a mesh axis runs over, the one named last changes fastest.
Arguments:
- features: bfloat16 [16, 16384, 256], P('snap', 'vert'), may hold values from -6 to 6
- tile_src: int32 [16, 1024], P('snap', 'vert'), may hold values from 0 to 127, as said below
- tile_dst: int32 [16, 1024], P('snap', 'vert'), may hold values from 0 to 127, as said below
- tile_count: int32 [16, 32], P('snap', 'vert'), may hold values from 4 to 32, as said below
- tile_vals: bfloat16 [16, 1024, 128, 128], P('snap', 'vert'), may hold values from -0.25 to 0.25
- norm_gain: float32 [256], replicated, may hold values from 0.25 to 1.75
- mix_weight: bfloat16 [256, 512], replicated, may hold values from -0.375 to 0.375
- decay_rate: float32 [16, 256], replicated, may hold values from 0 to 9, as said below
- mlp_gain: float32 [256], replicated, may hold values from 0.25 to 1.75
- up_weight: bfloat16 [256, 1024], replicated, may hold values from -0.375 to 0.375
- down_weight: bfloat16 [1024, 256], replicated, may hold values from -0.1875 to 0.1875
- link_weight: bfloat16 [256, 256], replicated, may hold values from -0.375 to 0.375
- pair_left: int32 [16, 1024], P('snap', 'vert'), may hold values from 0 to 127, as said below
- pair_right: int32 [16, 1024], P('snap', 'vert'), may hold values from 0 to 127, as said below
Outputs:
- embeddings: bfloat16 [16, 16384, 256], P('snap', 'vert')
- scores: bfloat16 [16, 1024, 128, 128], P('snap', 'vert')
Inputs may be any that keep to these rules, and one draw needn't show every extreme that they name: `tile_src`: a slot of vertex part p names a source block from p * 4 - 4 to p * 4 + 2 * 4 - 1. `tile_dst`: a slot of vertex part p names a destination block of that part, p * 4 to p * 4 + 3. `tile_count`: in every snapshot some vertex part has all 32 slots live. `decay_rate`: decay rates are positive. `pair_left`: a pair of vertex part p has its first block in that part, p * 4 to p * 4 + 3. `pair_right`: a pair of vertex part p has its second block from p * 4 - 4 to p * 4 + 2 * 4 - 1.
All inputs are finite; a program needn't handle non-finite values.
Results may differ from a plain program's by a relative error of at most 0.0091.
Values may be sent and summed in bfloat16 or wider, within the bound.
No kernel may reach another device: no remote copies, remote signals or barrier semaphores. Data moves between devices by JAX's collectives and lax.ppermute only.
A program may use at most 64 MiB of HBM per device.

v0:
```python
import jax
import jax.numpy as jnp
from jax import lax
from jax.sharding import PartitionSpec as P

epsilon = 1e-06


def with_halo(cells, sides, width):
    for axis, dim in sides:
        count = lax.axis_size(axis)
        ends = count - 1
        head = lax.slice_in_dim(cells, 0, width, axis=dim)
        tail = lax.slice_in_dim(cells, cells.shape[dim] - width, cells.shape[dim], axis=dim)
        cells = jnp.concatenate(
            [
                lax.ppermute(tail, axis, [(i, (i + 1) % count) for i in range(ends)]),
                cells,
                lax.ppermute(head, axis, [((i + 1) % count, i) for i in range(ends)]),
            ],
            axis=dim,
        )
    return cells


def root_norm(values, gain_vector):
    return (
        values
        * lax.rsqrt(jnp.mean(values * values, axis=-1, keepdims=True) + epsilon)
        * gain_vector
    )


def pick_blocks(blocks, indices):
    return jax.vmap(lambda source_table, chosen: jnp.take(source_table, chosen, axis=0))(
        blocks, indices
    )


def tile_terms(blocks, src_index, dst_index, tile_part, alive_slots, per_part):
    picked = pick_blocks(blocks, src_index)
    product = jnp.einsum("sgij,sgjf->sgif", tile_part, picked, preferred_element_type=jnp.float32)
    targets = jnp.arange(per_part, dtype=jnp.int32)[None, None, :]
    selector = ((dst_index[:, :, None] == targets) & alive_slots[:, :, None]).astype(jnp.float32)
    return jnp.einsum("sgb,sgif->sbif", selector, product, precision=lax.Precision.HIGHEST)


def gate_drive(normed, step_rates, mix_weight):
    projected = jnp.einsum("tnf,fg->tng", normed, mix_weight, preferred_element_type=jnp.float32)
    feature_width = normed.shape[-1]
    decays = jnp.exp(-step_rates[:, None, :] * jax.nn.sigmoid(projected[..., :feature_width]))
    return (decays, (1.0 - decays) * projected[..., feature_width:])


def advance(previous, inputs):
    updated = inputs[0] * previous + inputs[1]
    return (updated, updated)


def run_states(decays, drives, start_state):
    final_state, states = lax.scan(advance, start_state, (decays, drives))
    return states


def feed_forward(states, mlp_gain, up_weight, down_weight):
    state_normed = root_norm(states, mlp_gain).astype(jnp.bfloat16)
    hidden = jax.nn.silu(
        jnp.einsum("tnf,fh->tnh", state_normed, up_weight, preferred_element_type=jnp.float32)
    ).astype(jnp.bfloat16)
    return (
        states + jnp.einsum("tnh,hf->tnf", hidden, down_weight, preferred_element_type=jnp.float32)
    ).astype(jnp.bfloat16)


def body(
    features,
    tile_src,
    tile_dst,
    tile_count,
    tile_vals,
    norm_gain,
    mix_weight,
    decay_rate,
    mlp_gain,
    up_weight,
    down_weight,
    link_weight,
    pair_left,
    pair_right,
):
    snaps_here, vertices_here, feature_width = features.shape
    tile_rows = tile_vals.shape[-1]
    slot_count = tile_vals.shape[1]
    per_part = vertices_here // tile_rows
    part_index = lax.axis_index("vert")
    first_block = (part_index - 1) * per_part
    own_first = part_index * per_part
    extended = with_halo(features, (("vert", 1),), vertices_here)
    blocks = extended.reshape(snaps_here, 3 * per_part, tile_rows, feature_width)
    local_src = tile_src - first_block
    local_dst = tile_dst - own_first
    slot_ids = jnp.arange(slot_count, dtype=jnp.int32)[None, :]
    aggregate = tile_terms(blocks, local_src, local_dst, tile_vals, slot_ids < tile_count, per_part)
    combined = aggregate.reshape(snaps_here, vertices_here, feature_width) + features.astype(
        jnp.float32
    )
    normed = root_norm(combined, norm_gain).astype(jnp.bfloat16)
    by_vertex = lax.all_to_all(normed, "snap", split_axis=1, concat_axis=0, tiled=True)
    decays, drives = gate_drive(by_vertex, decay_rate, mix_weight)
    states = run_states(decays, drives, jnp.zeros(decays.shape[1:], jnp.float32))
    vertex_out = feed_forward(states, mlp_gain, up_weight, down_weight)
    embeddings = lax.all_to_all(vertex_out, "snap", split_axis=0, concat_axis=1, tiled=True)
    extended_out = with_halo(embeddings, (("vert", 1),), vertices_here)
    left_side = jnp.einsum(
        "svf,fg->svg", embeddings, link_weight, preferred_element_type=jnp.float32
    ).astype(jnp.bfloat16)
    left_blocks = pick_blocks(
        left_side.reshape(snaps_here, per_part, tile_rows, feature_width), pair_left - own_first
    )
    right_blocks = pick_blocks(
        extended_out.reshape(snaps_here, 3 * per_part, tile_rows, feature_width),
        pair_right - first_block,
    )
    scores = jnp.einsum(
        "spif,spjf->spij", left_blocks, right_blocks, preferred_element_type=jnp.float32
    ) * feature_width ** (-0.5)
    return (embeddings, scores.astype(jnp.bfloat16))


def solution(mesh):
    return jax.shard_map(
        body,
        mesh=mesh,
        in_specs=(
            P("snap", "vert", None),
            P("snap", "vert"),
            P("snap", "vert"),
            P("snap", "vert"),
            P("snap", "vert", None, None),
            P(),
            P(),
            P(),
            P(),
            P(),
            P(),
            P(),
            P("snap", "vert"),
            P("snap", "vert"),
        ),
        out_specs=(P("snap", "vert", None), P("snap", "vert", None, None)),
        check_vma=False,
    )
```

profile of v0, /device:TPU:97, one launch (start us, length us, event | category | flops | bytes accessed | tf_op | source)
XLA Modules:
  0.0 86.9 jit_solution(15219343378757450271)
XLA Ops:
  0.6 5.5 %collective-permute-start = (bf16[1,512,256]{2,1,0:T(8,128)(2,1)}, bf16[1,512,256]{2,1,0:T(8,128)(2,1)S(1)}, u32[]{:S(2)}, u32[]{:S(2)}) collective-permute-start(bf16[1,512,256]{2,1,0:T(8,128)(2,1)} %param.18), channel_id=1, source_target_pairs={{0,1},{1,2},{2,3},{3,4},{4,5},{5,6},{6,7},{7,8},{8,9},{9,10},{10,1... | collective-permute-start | bytes 786440 | tf_op jit(solution)/shard_map/ppermute | solution.py:17
  6.1 1.9 %collective-permute-start.1 = (bf16[1,512,256]{2,1,0:T(8,128)(2,1)}, bf16[1,512,256]{2,1,0:T(8,128)(2,1)S(1)}, u32[]{:S(2)}, u32[]{:S(2)}) collective-permute-start(bf16[1,512,256]{2,1,0:T(8,128)(2,1)} %param.18), channel_id=1, source_target_pairs={{1,0},{2,1},{3,2},{4,3},{5,4},{6,5},{7,6},{8,7},{9,8},{10,9},{11,1... | collective-permute-start | bytes 786440 | tf_op jit(solution)/shard_map/ppermute | solution.py:19
  8.0 0.7 and_bitcast_fusion.1
  10.0 0.7 neg.11
  10.8 4.4 %collective-permute-done.1 = bf16[1,512,256]{2,1,0:T(8,128)(2,1)S(1)} collective-permute-done((bf16[1,512,256]{2,1,0:T(8,128)(2,1)}, bf16[1,512,256]{2,1,0:T(8,128)(2,1)S(1)}, u32[]{:S(2)}, u32[]{:S(2)}) %collective-permute-start.1) | collective-permute-done | bytes 262176 | tf_op jit(solution)/shard_map/ppermute | solution.py:19
  15.2 1.0 %pad_maximum_fusion = bf16[1,1536,256]{2,1,0:T(8,128)(2,1)S(1)} fusion(bf16[1,512,256]{2,1,0:T(8,128)(2,1)S(1)} %collective-permute-done.1, bf16[1,512,256]{2,1,0:T(8,128)(2,1)} %param.18, bf16[1,512,256]{2,1,0:T(8,128)(2,1)S(1)} %collective-permute-done), kind=kLoop, calls=%fused_computation.27 | loop fusion | flops 2359296 | bytes 1572864 | tf_op jit(solution)/shard_map/concatenate | solution.py:15
  16.2 2.0 %gather_fusion.1 = bf16[32,128,256]{2,1,0:T(8,128)(2,1)} fusion(bf16[1,12,128,256]{3,2,1,0:T(8,128)(2,1)S(1)} %bitcast.104, s32[32]{0:T(128)S(1)} %or_bitcast_fusion.1), kind=kCustom, calls=%fused_computation.clone | custom fusion | bytes 4194560 | tf_op jit(solution)/shard_map/vmap(jit(_take))/gather | solution.py:35
  18.2 4.4 %convolution_bitcast_fusion = f32[32,128,256]{1,2,0:T(8,128)} fusion(bf16[32,128,256]{2,1,0:T(8,128)(2,1)} %gather_fusion.1, pred[32]{0:T(512)(128)(4,1)S(1)} %get-tuple-element.67, bf16[1,32,128,128]{3,2,1,0:T(8,128)(2,1)S(1)} %copy-done), kind=kOutput, calls=%fused_computation.6 | convolution fusion | flops 269484032 | bytes 7340064 | tf_op jit(solution)/shard_map/sgij,sgjf->sgif/dot_general | solution.py:42
  22.6 5.5 %copy.21 = f32[32,128,256]{2,0,1:T(8,128)} copy(f32[32,128,256]{1,2,0:T(8,128)} %convolution_bitcast_fusion) | data formatting | bytes 8388608 | tf_op jit(solution)/shard_map/sgij,sgjf->sgif/dot_general | solution.py:42
  28.1 3.7 %fusion.38 = f32[4,128,256]{2,0,1:T(4,128)S(1)} fusion(f32[32,128,256]{2,0,1:T(8,128)} %copy.21, s32[32]{0:T(128)S(1)} %subtract_bitcast_fusion, pred[32]{0:T(512)(128)(4,1)S(1)} %iota_compare_fusion.1), kind=kOutput, calls=%fused_computation.55 | convolution fusion | flops 50331904 | bytes 4718752 | tf_op jit(solution)/shard_map/sgb,sgif->sbif/dot_general | solution.py:45
  33.2 2.2 %reduce.1 = bf16[512,256]{1,0:T(8,128)(2,1)S(1)} reduce(bf16[512,1,256]{2,1,0:T(2,128)(2,1)S(1)} %bitcast.114, bf16[]{:T(256)} %broadcast.170), dimensions={1}, to_apply=%bitcast.97.reduce_sub_computation | reduce | bytes 524290
  35.4 0.8 reshape.205
  36.2 6.8 %all-to-all-start = ((bf16[16,2,4096]{2,1,0:T(2,128)(2,1)}), bf16[16,2,4096]{2,1,0:T(2,128)(2,1)S(1)}, u32[]{:S(2)}, u32[]{:S(2)}) async-start(bf16[16,2,4096]{2,1,0:T(2,128)(2,1)} %reshape.205), calls=%async_computation | async-start | bytes 524288 | tf_op jit(solution)/shard_map/all_to_all | solution.py:108
  43.0 7.3 %all-to-all-done = bf16[16,2,4096]{2,1,0:T(2,128)(2,1)S(1)} async-done(((bf16[16,2,4096]{2,1,0:T(2,128)(2,1)}), bf16[16,2,4096]{2,1,0:T(2,128)(2,1)S(1)}, u32[]{:S(2)}, u32[]{:S(2)}) %all-to-all-start) | async-done | bytes 262176 | tf_op jit(solution)/shard_map/all_to_all | solution.py:108
  52.0 2.8 %fusion.16 = bf16[16,32,256]{2,1,0:T(8,128)(2,1)} fusion(f32[16,32,256]{2,1,0:T(8,128)S(1)} %get-tuple-element.30, bf16[1024,256]{1,0:T(8,128)(2,1)} %param.28, bf16[256,1024]{1,0:T(8,128)(2,1)} %param.27, f32[256]{0:T(256)S(1)} %copy-done.7, f32[16,32]{1,0:T(8,128)S(1)} %add_rsqrt_fusion), kind=kOutput, calls=%fused_computation.20 | convolution fusion | flops 540147712 | bytes 1838080 | tf_op jit(solution)/shard_map/tnh,hf->tnf/dot_general | solution.py:71
  54.8 3.5 %all-to-all-start.1 = ((bf16[16,32,256]{2,1,0:T(8,128)(2,1)}), bf16[16,32,256]{2,1,0:T(8,128)(2,1)S(1)}, u32[]{:S(2)}, u32[]{:S(2)}) async-start(bf16[16,32,256]{2,1,0:T(8,128)(2,1)} %fusion.16), calls=%async_computation.1 | async-start | bytes 524288 | tf_op jit(solution)/shard_map/all_to_all | solution.py:112
  58.4 7.3 %all-to-all-done.1 = bf16[16,32,256]{2,1,0:T(8,128)(2,1)S(1)} async-done(((bf16[16,32,256]{2,1,0:T(8,128)(2,1)}), bf16[16,32,256]{2,1,0:T(8,128)(2,1)S(1)}, u32[]{:S(2)}, u32[]{:S(2)}) %all-to-all-start.1) | async-done | bytes 262176 | tf_op jit(solution)/shard_map/all_to_all | solution.py:112
  65.6 5.6 %collective-permute-start.2 = (bf16[1,512,256]{2,1,0:T(8,128)(2,1)S(1)}, bf16[1,512,256]{2,1,0:T(8,128)(2,1)S(1)}, u32[]{:S(2)}, u32[]{:S(2)}) collective-permute-start(bf16[1,512,256]{2,1,0:T(8,128)(2,1)S(1)} %bitcast.108), channel_id=1, source_target_pairs={{0,1},{1,2},{2,3},{3,4},{4,5},{5,6},{6,7},{7,8},{8,9},{9,10},{10,1... | collective-permute-start | bytes 786440 | tf_op jit(solution)/shard_map/ppermute | solution.py:17
  71.3 1.9 %collective-permute-start.3 = (bf16[1,512,256]{2,1,0:T(8,128)(2,1)S(1)}, bf16[1,512,256]{2,1,0:T(8,128)(2,1)S(1)}, u32[]{:S(2)}, u32[]{:S(2)}) collective-permute-start(bf16[1,512,256]{2,1,0:T(8,128)(2,1)S(1)} %bitcast.109), channel_id=1, source_target_pairs={{1,0},{2,1},{3,2},{4,3},{5,4},{6,5},{7,6},{8,7},{9,8},{10,9},{11,1... | collective-permute-start | bytes 786440 | tf_op jit(solution)/shard_map/ppermute | solution.py:19
  73.5 2.0 %gather_fusion = bf16[32,128,256]{2,1,0:T(8,128)(2,1)} fusion(bf16[1,4,128,256]{3,2,1,0:T(8,128)(2,1)S(1)} %bitcast.103, s32[32]{0:T(128)S(1)} %or_bitcast_fusion.2), kind=kCustom, calls=%fused_computation.2 | custom fusion | bytes 4194560 | tf_op jit(solution)/shard_map/vmap(jit(_take))/gather | solution.py:35
  75.5 4.7 %collective-permute-done.3 = bf16[1,512,256]{2,1,0:T(8,128)(2,1)S(1)} collective-permute-done((bf16[1,512,256]{2,1,0:T(8,128)(2,1)S(1)}, bf16[1,512,256]{2,1,0:T(8,128)(2,1)S(1)}, u32[]{:S(2)}, u32[]{:S(2)}) %collective-permute-start.3) | collective-permute-done | bytes 262176 | tf_op jit(solution)/shard_map/ppermute | solution.py:19
  80.2 2.0 %gather_fusion.2 = bf16[32,128,256]{2,1,0:T(8,128)(2,1)} fusion(bf16[1,12,128,256]{3,2,1,0:T(8,128)(2,1)S(1)} %bitcast.105, s32[32]{0:T(128)S(1)} %or_bitcast_fusion), kind=kCustom, calls=%fused_computation.1.clone | custom fusion | bytes 4194560 | tf_op jit(solution)/shard_map/vmap(jit(_take))/gather | solution.py:35
  82.2 4.0 %fusion.11 = bf16[1,32,128,128]{3,2,1,0:T(8,128)(2,1)} fusion(bf16[32,128,256]{2,1,0:T(8,128)(2,1)} %gather_fusion.2, pred[32]{0:T(512)(128)(4,1)S(1)} %get-tuple-element.63, bf16[32,128,256]{2,1,0:T(8,128)(2,1)} %gather_fusion, pred[32]{0:T(512)(128)(4,1)S(1)} %get-tuple-element.69), kind=kOutput, calls=%fused_computation.18 | convolution fusion | flops 271581184 | bytes 5242944 | tf_op jit(solution)/shard_map/spif,spjf->spij/dot_general | solution.py:124
  86.2 0.7 copy.40
  (60 shorter events, 4.3 us)
Async XLA Ops:
  0.6 17.6 %copy-start = (bf16[1,32,128,128]{3,2,1,0:T(8,128)(2,1)S(1)}, bf16[1,32,128,128]{3,2,1,0:T(8,128)(2,1)}, u32[]{:S(2)}) copy-start(bf16[1,32,128,128]{3,2,1,0:T(8,128)(2,1)} %param.22) | copy-start | bytes 3145732
  0.6 10.1 %collective-permute-start = (bf16[1,512,256]{2,1,0:T(8,128)(2,1)}, bf16[1,512,256]{2,1,0:T(8,128)(2,1)S(1)}, u32[]{:S(2)}, u32[]{:S(2)}) collective-permute-start(bf16[1,512,256]{2,1,0:T(8,128)(2,1)} %param.18), channel_id=1, source_target_pairs={{0,1},{1,2},{2,3},{3,4},{4,5},{5,6},{6,7},{7,8},{8,9},{9,10},{10,1... | collective-permute-start | bytes 786440 | tf_op jit(solution)/shard_map/ppermute | solution.py:17
  6.1 9.1 %collective-permute-start.1 = (bf16[1,512,256]{2,1,0:T(8,128)(2,1)}, bf16[1,512,256]{2,1,0:T(8,128)(2,1)S(1)}, u32[]{:S(2)}, u32[]{:S(2)}) collective-permute-start(bf16[1,512,256]{2,1,0:T(8,128)(2,1)} %param.18), channel_id=1, source_target_pairs={{1,0},{2,1},{3,2},{4,3},{5,4},{6,5},{7,6},{8,7},{9,8},{10,9},{11,1... | collective-permute-start | bytes 786440 | tf_op jit(solution)/shard_map/ppermute | solution.py:19
  28.1 3.8 %copy-start.1 = (bf16[1,512,256]{2,1,0:T(8,128)(2,1)S(1)}, bf16[1,512,256]{2,1,0:T(8,128)(2,1)}, u32[]{:S(2)}) copy-start(bf16[1,512,256]{2,1,0:T(8,128)(2,1)} %param.18) | copy-start | bytes 786436
  28.1 4.0 %copy-start.4 = (f32[256]{0:T(256)S(1)}, f32[256]{0:T(256)}, u32[]{:S(2)}) copy-start(f32[256]{0:T(256)} %param.23) | copy-start | bytes 3076
  31.9 11.1 %copy-start.5 = (s32[1,32]{1,0:T(1,128)S(1)}, s32[1,32]{1,0:T(1,128)}, u32[]{:S(2)}) copy-start(s32[1,32]{1,0:T(1,128)} %param.31) | copy-start | bytes 388
  31.9 11.1 %copy-start.6 = (s32[1,32]{1,0:T(1,128)S(1)}, s32[1,32]{1,0:T(1,128)}, u32[]{:S(2)}) copy-start(s32[1,32]{1,0:T(1,128)} %param.30) | copy-start | bytes 388
  32.2 18.3 %copy-start.2 = (bf16[256,512]{1,0:T(8,128)(2,1)S(1)}, bf16[256,512]{1,0:T(8,128)(2,1)}, u32[]{:S(2)}) copy-start(bf16[256,512]{1,0:T(8,128)(2,1)} %param.24) | copy-start | bytes 786436
  36.2 14.1 %all-to-all-start = ((bf16[16,2,4096]{2,1,0:T(2,128)(2,1)}), bf16[16,2,4096]{2,1,0:T(2,128)(2,1)S(1)}, u32[]{:S(2)}, u32[]{:S(2)}) async-start(bf16[16,2,4096]{2,1,0:T(2,128)(2,1)} %reshape.205), calls=%async_computation | async-start | bytes 524288 | tf_op jit(solution)/shard_map/all_to_all | solution.py:108
  50.9 1.1 %copy-start.7 = (f32[256]{0:T(256)S(1)}, f32[256]{0:T(256)}, u32[]{:S(2)}) copy-start(f32[256]{0:T(256)} %param.26) | copy-start | bytes 3076
  52.0 21.3 %copy-start.3 = (bf16[256,256]{1,0:T(8,128)(2,1)S(1)}, bf16[256,256]{1,0:T(8,128)(2,1)}, u32[]{:S(2)}) copy-start(bf16[256,256]{1,0:T(8,128)(2,1)} %param.29) | copy-start | bytes 393220
  54.8 10.8 %all-to-all-start.1 = ((bf16[16,32,256]{2,1,0:T(8,128)(2,1)}), bf16[16,32,256]{2,1,0:T(8,128)(2,1)S(1)}, u32[]{:S(2)}, u32[]{:S(2)}) async-start(bf16[16,32,256]{2,1,0:T(8,128)(2,1)} %fusion.16), calls=%async_computation.1 | async-start | bytes 524288 | tf_op jit(solution)/shard_map/all_to_all | solution.py:112
  65.6 9.8 %collective-permute-start.2 = (bf16[1,512,256]{2,1,0:T(8,128)(2,1)S(1)}, bf16[1,512,256]{2,1,0:T(8,128)(2,1)S(1)}, u32[]{:S(2)}, u32[]{:S(2)}) collective-permute-start(bf16[1,512,256]{2,1,0:T(8,128)(2,1)S(1)} %bitcast.108), channel_id=1, source_target_pairs={{0,1},{1,2},{2,3},{3,4},{4,5},{5,6},{6,7},{7,8},{8,9},{9,10},{10,1... | collective-permute-start | bytes 786440 | tf_op jit(solution)/shard_map/ppermute | solution.py:17
  71.3 8.9 %collective-permute-start.3 = (bf16[1,512,256]{2,1,0:T(8,128)(2,1)S(1)}, bf16[1,512,256]{2,1,0:T(8,128)(2,1)S(1)}, u32[]{:S(2)}, u32[]{:S(2)}) collective-permute-start(bf16[1,512,256]{2,1,0:T(8,128)(2,1)S(1)} %bitcast.109), channel_id=1, source_target_pairs={{1,0},{2,1},{3,2},{4,3},{5,4},{6,5},{7,6},{8,7},{9,8},{10,9},{11,1... | collective-permute-start | bytes 786440 | tf_op jit(solution)/shard_map/ppermute | solution.py:19
where the time goes:
time: 87.6 us; the launch traced here: 86.9 us
  starting transfers between devices  25.2 us (29%)
  waiting for transfers between devices  23.7 us (27%)
  matrix products  15.4 us (18%)
  local copies, waits for them, and re-layouts  14.4 us (16%)
  other arithmetic  6.3 us (7%)
  between operations  1.6 us (2%)
    ppermute x2, starting transfers between devices, with_halo(): lax.ppermute(tail, axis, [(i, (i + 1) % count) for i in range(ends)])  11.1 us
    ppermute x2, waiting for transfers between devices, with_halo(): lax.ppermute(head, axis, [((i + 1) % count, i) for i in range(ends)])  9.16 us
    all_to_all x1, waiting for transfers between devices, body(): lax.all_to_all(vertex_out, 'snap', split_axis=0, concat_axis=1, tiled=True)  7.28 us
    all_to_all x1, waiting for transfers between devices, body(): lax.all_to_all(normed, 'snap', split_axis=1, concat_axis=0, tiled=True)  7.26 us
    all_to_all x1, starting transfers between devices, body(): lax.all_to_all(normed, 'snap', split_axis=1, concat_axis=0, tiled=True)  6.75 us
    gather x6, local copies, waits for them, and re-layouts, pick_blocks(): jnp.take(source_table, chosen, axis=0)  6.03 us
    dot_general x1, local copies, waits for them, and re-layouts, tile_terms(): jnp.einsum('sgij,sgjf->sgif', tile_part, picked, preferred_element_type=j...  5.47 us
    dot_general x1, matrix products, tile_terms(): jnp.einsum('sgij,sgjf->sgif', tile_part, picked, preferred_element_type=j...  4.37 us
  transfers between devices with their start and end apart: 6, of which 4 were waited for; matrix products, arithmetic and copies ran while one was open for 5% of the time, Pallas kernels for 0%

commit v1 on v0

--- a/solution.py
+++ b/solution.py
@@ -105,7 +105,10 @@
         jnp.float32
     )
     normed = root_norm(combined, norm_gain).astype(jnp.bfloat16)
-    by_vertex = lax.all_to_all(normed, "snap", split_axis=1, concat_axis=0, tiled=True)
+    by_vertex = jnp.concatenate(
+        lax.all_to_all(jnp.stack(jnp.split(normed, lax.axis_size("snap"), axis=1)), "snap", 0, 0),
+        axis=0,
+    )
     decays, drives = gate_drive(by_vertex, decay_rate, mix_weight)
     states = run_states(decays, drives, jnp.zeros(decays.shape[1:], jnp.float32))
     vertex_out = feed_forward(states, mlp_gain, up_weight, down_weight)

time: 87.6 us -> 93.1 us (1.063)
  local copies, waits for them, and re-layouts: 14.4 us -> 22.1 us
  other arithmetic: 6.3 us -> 4.09 us
    unnamed x21 -> x32, local copies, waits for them, and re-layouts: 2.34 us -> 9.85 us
    unnamed x2 -> x1, other arithmetic: 2.21 us -> 0.01 us
where the time goes in v1:
time: 93.1 us; the launch traced here: 92.4 us
  starting transfers between devices  25.2 us (27%)
  waiting for transfers between devices  23.7 us (25%)
  local copies, waits for them, and re-layouts  22.1 us (24%)
  matrix products  15.4 us (17%)
  other arithmetic  4.09 us (4%)
  between operations  1.56 us (2%)
    ppermute x2, starting transfers between devices, with_halo(): lax.ppermute(tail, axis, [(i, (i + 1) % count) for i in range(ends)])  11.1 us
    unnamed x32, local copies, waits for them, and re-layouts  9.85 us
    ppermute x2, waiting for transfers between devices, with_halo(): lax.ppermute(head, axis, [((i + 1) % count, i) for i in range(ends)])  9.16 us
    all_to_all x1, waiting for transfers between devices, body(): lax.all_to_all(vertex_out, 'snap', split_axis=0, concat_axis=1, tiled=True)  7.28 us
    all_to_all x1, waiting for transfers between devices, body(): lax.all_to_all(jnp.stack(jnp.split(normed, lax.axis_size('snap'), axis=1)...  7.26 us
    all_to_all x1, starting transfers between devices, body(): lax.all_to_all(jnp.stack(jnp.split(normed, lax.axis_size('snap'), axis=1)...  6.75 us
    gather x6, local copies, waits for them, and re-layouts, pick_blocks(): jnp.take(source_table, chosen, axis=0)  6.06 us
    dot_general x1, local copies, waits for them, and re-layouts, tile_terms(): jnp.einsum('sgij,sgjf->sgif', tile_part, picked, preferred_element_type=j...  5.48 us
  transfers between devices with their start and end apart: 6, of which 4 were waited for; matrix products, arithmetic and copies ran while one was open for 5% of the time, Pallas kernels for 0%

profile of v1, /device:TPU:97, one launch (start us, length us, event | category | flops | bytes accessed | tf_op | source)
XLA Modules:
  0.0 92.4 jit_solution(9433325267545814258)
XLA Ops:
  0.6 5.5 %collective-permute-start = (bf16[1,512,256]{2,1,0:T(8,128)(2,1)}, bf16[1,512,256]{2,1,0:T(8,128)(2,1)S(1)}, u32[]{:S(2)}, u32[]{:S(2)}) collective-permute-start(bf16[1,512,256]{2,1,0:T(8,128)(2,1)} %param.18), channel_id=1, source_target_pairs={{0,1},{1,2},{2,3},{3,4},{4,5},{5,6},{6,7},{7,8},{8,9},{9,10},{10,1... | collective-permute-start | bytes 786440 | tf_op jit(solution)/shard_map/ppermute | solution.py:17
  6.1 1.9 %collective-permute-start.1 = (bf16[1,512,256]{2,1,0:T(8,128)(2,1)}, bf16[1,512,256]{2,1,0:T(8,128)(2,1)S(1)}, u32[]{:S(2)}, u32[]{:S(2)}) collective-permute-start(bf16[1,512,256]{2,1,0:T(8,128)(2,1)} %param.18), channel_id=1, source_target_pairs={{1,0},{2,1},{3,2},{4,3},{5,4},{6,5},{7,6},{8,7},{9,8},{10,9},{11,1... | collective-permute-start | bytes 786440 | tf_op jit(solution)/shard_map/ppermute | solution.py:19
  8.0 0.7 and_bitcast_fusion.1
  9.4 0.7 subtract_bitcast_fusion
  10.0 0.7 neg.11
  10.8 4.4 %collective-permute-done.1 = bf16[1,512,256]{2,1,0:T(8,128)(2,1)S(1)} collective-permute-done((bf16[1,512,256]{2,1,0:T(8,128)(2,1)}, bf16[1,512,256]{2,1,0:T(8,128)(2,1)S(1)}, u32[]{:S(2)}, u32[]{:S(2)}) %collective-permute-start.1) | collective-permute-done | bytes 262176 | tf_op jit(solution)/shard_map/ppermute | solution.py:19
  15.2 1.0 %pad_maximum_fusion = bf16[1,1536,256]{2,1,0:T(8,128)(2,1)S(1)} fusion(bf16[1,512,256]{2,1,0:T(8,128)(2,1)S(1)} %collective-permute-done.1, bf16[1,512,256]{2,1,0:T(8,128)(2,1)} %param.18, bf16[1,512,256]{2,1,0:T(8,128)(2,1)S(1)} %collective-permute-done), kind=kLoop, calls=%fused_computation.27 | loop fusion | flops 2359296 | bytes 1572864 | tf_op jit(solution)/shard_map/concatenate | solution.py:15
  16.2 2.0 %gather_fusion.1 = bf16[32,128,256]{2,1,0:T(8,128)(2,1)} fusion(bf16[1,12,128,256]{3,2,1,0:T(8,128)(2,1)S(1)} %bitcast.165, s32[32]{0:T(128)S(1)} %or_bitcast_fusion.1), kind=kCustom, calls=%fused_computation.clone | custom fusion | bytes 4194560 | tf_op jit(solution)/shard_map/vmap(jit(_take))/gather | solution.py:35
  18.2 4.4 %convolution_bitcast_fusion = f32[32,128,256]{1,2,0:T(8,128)} fusion(bf16[32,128,256]{2,1,0:T(8,128)(2,1)} %gather_fusion.1, pred[32]{0:T(512)(128)(4,1)S(1)} %get-tuple-element.67, bf16[1,32,128,128]{3,2,1,0:T(8,128)(2,1)S(1)} %copy-done), kind=kOutput, calls=%fused_computation.6 | convolution fusion | flops 269484032 | bytes 7340064 | tf_op jit(solution)/shard_map/sgij,sgjf->sgif/dot_general | solution.py:42
  22.6 5.5 %copy.50 = f32[32,128,256]{2,0,1:T(8,128)} copy(f32[32,128,256]{1,2,0:T(8,128)} %convolution_bitcast_fusion) | data formatting | bytes 8388608 | tf_op jit(solution)/shard_map/sgij,sgjf->sgif/dot_general | solution.py:42
  28.1 3.7 %fusion.39 = f32[4,128,256]{2,0,1:T(4,128)S(1)} fusion(f32[32,128,256]{2,0,1:T(8,128)} %copy.50, s32[32]{0:T(128)S(1)} %subtract_bitcast_fusion, pred[32]{0:T(512)(128)(4,1)S(1)} %iota_compare_fusion.1), kind=kOutput, calls=%fused_computation.88 | convolution fusion | flops 50331904 | bytes 4718752 | tf_op jit(solution)/shard_map/sgb,sgif->sbif/dot_general | solution.py:45
  42.0 6.8 %all-to-all-start = ((bf16[16,1,32,256]{3,2,1,0:T(8,128)(2,1)}), bf16[16,1,32,256]{3,2,1,0:T(8,128)(2,1)S(1)}, u32[]{:S(2)}, u32[]{:S(2)}) async-start(bf16[16,1,32,256]{3,2,1,0:T(8,128)(2,1)} %constant_dynamic-update-slice_fusion), calls=%async_computation | async-start | bytes 524288 | tf_op jit(solution)/shard_map/all_to_all | solution.py:109
  48.8 7.3 %all-to-all-done = bf16[16,1,32,256]{3,2,1,0:T(8,128)(2,1)S(1)} async-done(((bf16[16,1,32,256]{3,2,1,0:T(8,128)(2,1)}), bf16[16,1,32,256]{3,2,1,0:T(8,128)(2,1)S(1)}, u32[]{:S(2)}, u32[]{:S(2)}) %all-to-all-start) | async-done | bytes 262176 | tf_op jit(solution)/shard_map/all_to_all | solution.py:109
  56.6 0.6 while.13
  57.5 2.8 %fusion.16 = bf16[16,32,256]{2,1,0:T(8,128)(2,1)} fusion(f32[16,32,256]{2,1,0:T(8,128)S(1)} %get-tuple-element.30, bf16[1024,256]{1,0:T(8,128)(2,1)} %param.28, bf16[256,1024]{1,0:T(8,128)(2,1)} %param.27, f32[256]{0:T(256)S(1)} %copy-done.7, f32[16,32]{1,0:T(8,128)S(1)} %add_rsqrt_fusion), kind=kOutput, calls=%fused_computation.20 | convolution fusion | flops 540147712 | bytes 1838080 | tf_op jit(solution)/shard_map/tnh,hf->tnf/dot_general | solution.py:71
  60.3 3.5 %all-to-all-start.1 = ((bf16[16,32,256]{2,1,0:T(8,128)(2,1)}), bf16[16,32,256]{2,1,0:T(8,128)(2,1)S(1)}, u32[]{:S(2)}, u32[]{:S(2)}) async-start(bf16[16,32,256]{2,1,0:T(8,128)(2,1)} %fusion.16), calls=%async_computation.1 | async-start | bytes 524288 | tf_op jit(solution)/shard_map/all_to_all | solution.py:115
  63.8 7.3 %all-to-all-done.1 = bf16[16,32,256]{2,1,0:T(8,128)(2,1)S(1)} async-done(((bf16[16,32,256]{2,1,0:T(8,128)(2,1)}), bf16[16,32,256]{2,1,0:T(8,128)(2,1)S(1)}, u32[]{:S(2)}, u32[]{:S(2)}) %all-to-all-start.1) | async-done | bytes 262176 | tf_op jit(solution)/shard_map/all_to_all | solution.py:115
  71.1 5.6 %collective-permute-start.2 = (bf16[1,512,256]{2,1,0:T(8,128)(2,1)S(1)}, bf16[1,512,256]{2,1,0:T(8,128)(2,1)S(1)}, u32[]{:S(2)}, u32[]{:S(2)}) collective-permute-start(bf16[1,512,256]{2,1,0:T(8,128)(2,1)S(1)} %bitcast.169), channel_id=1, source_target_pairs={{0,1},{1,2},{2,3},{3,4},{4,5},{5,6},{6,7},{7,8},{8,9},{9,10},{10,1... | collective-permute-start | bytes 786440 | tf_op jit(solution)/shard_map/ppermute | solution.py:17
  76.8 1.9 %collective-permute-start.3 = (bf16[1,512,256]{2,1,0:T(8,128)(2,1)S(1)}, bf16[1,512,256]{2,1,0:T(8,128)(2,1)S(1)}, u32[]{:S(2)}, u32[]{:S(2)}) collective-permute-start(bf16[1,512,256]{2,1,0:T(8,128)(2,1)S(1)} %bitcast.170), channel_id=1, source_target_pairs={{1,0},{2,1},{3,2},{4,3},{5,4},{6,5},{7,6},{8,7},{9,8},{10,9},{11,1... | collective-permute-start | bytes 786440 | tf_op jit(solution)/shard_map/ppermute | solution.py:19
  79.0 2.0 %gather_fusion = bf16[32,128,256]{2,1,0:T(8,128)(2,1)} fusion(bf16[1,4,128,256]{3,2,1,0:T(8,128)(2,1)S(1)} %bitcast.164, s32[32]{0:T(128)S(1)} %or_bitcast_fusion.2), kind=kCustom, calls=%fused_computation.2 | custom fusion | bytes 4194560 | tf_op jit(solution)/shard_map/vmap(jit(_take))/gather | solution.py:35
  81.0 4.7 %collective-permute-done.3 = bf16[1,512,256]{2,1,0:T(8,128)(2,1)S(1)} collective-permute-done((bf16[1,512,256]{2,1,0:T(8,128)(2,1)S(1)}, bf16[1,512,256]{2,1,0:T(8,128)(2,1)S(1)}, u32[]{:S(2)}, u32[]{:S(2)}) %collective-permute-start.3) | collective-permute-done | bytes 262176 | tf_op jit(solution)/shard_map/ppermute | solution.py:19
  85.7 2.0 %gather_fusion.2 = bf16[32,128,256]{2,1,0:T(8,128)(2,1)} fusion(bf16[1,12,128,256]{3,2,1,0:T(8,128)(2,1)S(1)} %bitcast.166, s32[32]{0:T(128)S(1)} %or_bitcast_fusion), kind=kCustom, calls=%fused_computation.1.clone | custom fusion | bytes 4194560 | tf_op jit(solution)/shard_map/vmap(jit(_take))/gather | solution.py:35
  87.7 4.0 %fusion.11 = bf16[1,32,128,128]{3,2,1,0:T(8,128)(2,1)} fusion(bf16[32,128,256]{2,1,0:T(8,128)(2,1)} %gather_fusion.2, pred[32]{0:T(512)(128)(4,1)S(1)} %get-tuple-element.63, bf16[32,128,256]{2,1,0:T(8,128)(2,1)} %gather_fusion, pred[32]{0:T(512)(128)(4,1)S(1)} %get-tuple-element.69), kind=kOutput, calls=%fused_computation.18 | convolution fusion | flops 271581184 | bytes 5242944 | tf_op jit(solution)/shard_map/spif,spjf->spij/dot_general | solution.py:127
  91.7 0.7 copy.80
  (70 shorter events, 11.4 us)
Async XLA Ops:
  0.6 17.6 %copy-start = (bf16[1,32,128,128]{3,2,1,0:T(8,128)(2,1)S(1)}, bf16[1,32,128,128]{3,2,1,0:T(8,128)(2,1)}, u32[]{:S(2)}) copy-start(bf16[1,32,128,128]{3,2,1,0:T(8,128)(2,1)} %param.22) | copy-start | bytes 3145732
  0.6 10.1 %collective-permute-start = (bf16[1,512,256]{2,1,0:T(8,128)(2,1)}, bf16[1,512,256]{2,1,0:T(8,128)(2,1)S(1)}, u32[]{:S(2)}, u32[]{:S(2)}) collective-permute-start(bf16[1,512,256]{2,1,0:T(8,128)(2,1)} %param.18), channel_id=1, source_target_pairs={{0,1},{1,2},{2,3},{3,4},{4,5},{5,6},{6,7},{7,8},{8,9},{9,10},{10,1... | collective-permute-start | bytes 786440 | tf_op jit(solution)/shard_map/ppermute | solution.py:17
  6.1 9.1 %collective-permute-start.1 = (bf16[1,512,256]{2,1,0:T(8,128)(2,1)}, bf16[1,512,256]{2,1,0:T(8,128)(2,1)S(1)}, u32[]{:S(2)}, u32[]{:S(2)}) collective-permute-start(bf16[1,512,256]{2,1,0:T(8,128)(2,1)} %param.18), channel_id=1, source_target_pairs={{1,0},{2,1},{3,2},{4,3},{5,4},{6,5},{7,6},{8,7},{9,8},{10,9},{11,1... | collective-permute-start | bytes 786440 | tf_op jit(solution)/shard_map/ppermute | solution.py:19
  28.1 3.8 %copy-start.1 = (bf16[1,512,256]{2,1,0:T(8,128)(2,1)S(1)}, bf16[1,512,256]{2,1,0:T(8,128)(2,1)}, u32[]{:S(2)}) copy-start(bf16[1,512,256]{2,1,0:T(8,128)(2,1)} %param.18) | copy-start | bytes 786436
  28.1 4.0 %copy-start.4 = (f32[256]{0:T(256)S(1)}, f32[256]{0:T(256)}, u32[]{:S(2)}) copy-start(f32[256]{0:T(256)} %param.23) | copy-start | bytes 3076
  31.8 17.0 %copy-start.5 = (s32[1,32]{1,0:T(1,128)S(1)}, s32[1,32]{1,0:T(1,128)}, u32[]{:S(2)}) copy-start(s32[1,32]{1,0:T(1,128)} %param.31) | copy-start | bytes 388
  31.8 17.0 %copy-start.6 = (s32[1,32]{1,0:T(1,128)S(1)}, s32[1,32]{1,0:T(1,128)}, u32[]{:S(2)}) copy-start(s32[1,32]{1,0:T(1,128)} %param.30) | copy-start | bytes 388
  31.8 24.3 %copy-start.2 = (bf16[256,512]{1,0:T(8,128)(2,1)S(1)}, bf16[256,512]{1,0:T(8,128)(2,1)}, u32[]{:S(2)}) copy-start(bf16[256,512]{1,0:T(8,128)(2,1)} %param.24) | copy-start | bytes 786436
  42.0 14.1 %all-to-all-start = ((bf16[16,1,32,256]{3,2,1,0:T(8,128)(2,1)}), bf16[16,1,32,256]{3,2,1,0:T(8,128)(2,1)S(1)}, u32[]{:S(2)}, u32[]{:S(2)}) async-start(bf16[16,1,32,256]{3,2,1,0:T(8,128)(2,1)} %constant_dynamic-update-slice_fusion), calls=%async_computation | async-start | bytes 524288 | tf_op jit(solution)/shard_map/all_to_all | solution.py:109
  56.4 1.1 %copy-start.7 = (f32[256]{0:T(256)S(1)}, f32[256]{0:T(256)}, u32[]{:S(2)}) copy-start(f32[256]{0:T(256)} %param.26) | copy-start | bytes 3076
  57.5 21.3 %copy-start.3 = (bf16[256,256]{1,0:T(8,128)(2,1)S(1)}, bf16[256,256]{1,0:T(8,128)(2,1)}, u32[]{:S(2)}) copy-start(bf16[256,256]{1,0:T(8,128)(2,1)} %param.29) | copy-start | bytes 393220
  60.3 10.8 %all-to-all-start.1 = ((bf16[16,32,256]{2,1,0:T(8,128)(2,1)}), bf16[16,32,256]{2,1,0:T(8,128)(2,1)S(1)}, u32[]{:S(2)}, u32[]{:S(2)}) async-start(bf16[16,32,256]{2,1,0:T(8,128)(2,1)} %fusion.16), calls=%async_computation.1 | async-start | bytes 524288 | tf_op jit(solution)/shard_map/all_to_all | solution.py:115
  71.1 9.8 %collective-permute-start.2 = (bf16[1,512,256]{2,1,0:T(8,128)(2,1)S(1)}, bf16[1,512,256]{2,1,0:T(8,128)(2,1)S(1)}, u32[]{:S(2)}, u32[]{:S(2)}) collective-permute-start(bf16[1,512,256]{2,1,0:T(8,128)(2,1)S(1)} %bitcast.169), channel_id=1, source_target_pairs={{0,1},{1,2},{2,3},{3,4},{4,5},{5,6},{6,7},{7,8},{8,9},{9,10},{10,1... | collective-permute-start | bytes 786440 | tf_op jit(solution)/shard_map/ppermute | solution.py:17
  76.8 8.9 %collective-permute-start.3 = (bf16[1,512,256]{2,1,0:T(8,128)(2,1)S(1)}, bf16[1,512,256]{2,1,0:T(8,128)(2,1)S(1)}, u32[]{:S(2)}, u32[]{:S(2)}) collective-permute-start(bf16[1,512,256]{2,1,0:T(8,128)(2,1)S(1)} %bitcast.170), channel_id=1, source_target_pairs={{1,0},{2,1},{3,2},{4,3},{5,4},{6,5},{7,6},{8,7},{9,8},{10,9},{11,1... | collective-permute-start | bytes 786440 | tf_op jit(solution)/shard_map/ppermute | solution.py:19
